TPU v7x, 128 devices: a whole 4x4x4 slice. The times are simulated.
128 devices in a mesh: dev: 128 (over z, y, x, core).
Axes of the slice: x: 4, y: 4, z: 4, core: 2. Of those that a mesh axis runs over, the one named last changes fastest.
Arguments:
- leaves: float32 [2, 1000, 59392], P(None, None, 'dev'), may hold values from -6 to 6
- send_slot: int32 [4, 32768], P(None, 'dev'), may hold values from 0 to 128, as said below
- recv_slot: int32 [4, 32768], P(None, 'dev'), may hold values from 0 to 128, as said below
- filter_up: float32 [20, 20], replicated, may hold values from -1 to 1.05
- filter_down: float32 [20, 20], replicated, may hold values from -1 to 1.05
Outputs:
- leaves_out: float32 [2, 1000, 59392], P(None, None, 'dev')
Inputs may be any that keep to these rules, and one draw needn't show every extreme that they name: `send_slot`: for each level and each device's block of 256 entries, every local child 0 .. 127 stands in exactly one slot and all other slots hold 128; the number of children one device sends to one device at one level varies from pair to pair and reaches 2 in every level. `recv_slot`: for each level and each device's block of 256 entries, the slots that its sources fill hold each of 0 .. 127 exactly once, and exactly the empty slots hold 128.
All inputs are finite; a program needn't handle non-finite values.
Results may differ from a plain program's by a relative error of at most 0.0001.
Values sent between devices are 32-bit elements; how exact they have to be, the bound alone decides.
No kernel may reach another device: no remote copies, remote signals or barrier semaphores. Data moves between devices by JAX's collectives and lax.ppermute only.
A program may use at most 128 MiB of HBM per device.

v0:
```python
import functools

import jax
import jax.numpy as jnp
from jax import lax
from jax.experimental import pallas as pl
from jax.experimental.pallas import tpu as pltpu
from jax.sharding import PartitionSpec as P

PER = 128
PARENTS = 16
DEGREE = 10
CELLS = 1000
PLANE = 100
SLOTS = 256
GROUPS = ((0, 1),)
COUNT = len(GROUPS[0])
HEIGHT = 8 * COUNT
ROWS = PARENTS
WIDE = COUNT * 20 * ROWS
LIMIT = 50_000_000
FULL = 63_400_000
TAKE = 0
PLACE = 4
UP_ROW, BOTH_ROW, DOWN_ROW, PLANE_ROW, DOWN_PLANE, BANK_USED = (0, 320, 960, 1600, 2624, 2880)
BANK = 8448
SPLITS = 10496
LEVEL_ROOM = 12 // COUNT
BASE_ROOM = 18 // COUNT

highest = lax.Precision.HIGHEST
f32 = jnp.float32
bf16 = jnp.bfloat16
VMEM = pl.BlockSpec(memory_space=pltpu.VMEM)
SMEM = pl.BlockSpec(memory_space=pltpu.SMEM)
HBM = pl.BlockSpec(memory_space=pltpu.HBM)
DMA = pltpu.SemaphoreType.DMA


def leaf_range(height):
    if height == 0:
        return (0, PER)
    return (PER + 7 * PARENTS * (height - 1), 7 * PARENTS)


def split(value):
    high = value.astype(bf16)
    return high, (value - high.astype(f32)).astype(bf16)


def product(left, right):
    dot = functools.partial(jnp.dot, preferred_element_type=f32)
    return dot(left[0], right[0]) + (dot(left[0], right[1]) + dot(left[1], right[0]))


def windows(chunks):
    lane = lax.broadcasted_iota(jnp.int32, (ROWS, 128), 1)
    result = []
    for i in range(DEGREE):
        first, offset = divmod(PLANE * i, 128)
        value = chunks[first]
        if offset:
            value = pltpu.roll(value, 128 - offset, 1)
            if offset + PLANE > 128:
                later = pltpu.roll(chunks[first + 1], 128 - offset, 1)
                value = jnp.where(lane < 128 - offset, value, later)
        result.append(value)
    return result


def merge(parts):
    lane = lax.broadcasted_iota(jnp.int32, (ROWS, 128), 1)
    result = []
    for part in range(8):
        value = None
        for i in range(DEGREE):
            start = PLANE * i - 128 * part
            if start >= 128 or start + PLANE <= 0:
                continue
            piece = parts[i]
            if start % 128:
                piece = pltpu.roll(piece, start % 128, 1)
            if value is None:
                value = piece
            else:
                value = jnp.where(lane < start, value, piece)
        if part == 7:
            value = jnp.where(lane < CELLS - 896, value, 0.0)
        result.append(value)
    return result


def pack_rows(rows, start, number, flat_ref):
    for first in range(start, start + number, 8):
        for n in range(COUNT):
            for part in range(8):
                if part < 7:
                    value = rows[n, first : first + 8, 128 * part : 128 * part + 128]
                else:
                    value = rows[n, first : first + 8, 896:CELLS]
                    value = jnp.concatenate([value, jnp.zeros((8, 1024 - CELLS), f32)], axis=1)
                flat_ref[pl.ds(first * HEIGHT + n * 8 + part, 8, stride=HEIGHT), :] = value


def block(flat, index):
    return flat[index * HEIGHT : (index + 1) * HEIGHT, :]


def fetch(pairs, sems):
    copies = [pltpu.make_async_copy(source, target, sems.at[i]) for i, (source, target) in enumerate(pairs)]
    for copy in copies:
        copy.start()
    return copies


def first_kernel(orbital, send_ref, leaves_ref, out_ref, send, rows, flat, filled, sems):
    quarter = PER // 4
    pairs = [(send_ref, send)]
    for i in range(4):
        span = slice(i * quarter, (i + 1) * quarter)
        pairs.append((leaves_ref.at[orbital : orbital + COUNT, span, :], rows.at[:, span, :]))
    copies = fetch(pairs, sems)
    for i in range(4):
        copies[i + 1].wait()
        pack_rows(rows, i * quarter, quarter, flat)
    copies[0].wait()
    outs = []
    quarter = SLOTS // 4
    for i in range(4):
        for slot in range(i * quarter, (i + 1) * quarter):
            start = pl.multiple_of(jnp.minimum(send[0, slot], PER - 1) * HEIGHT, HEIGHT)
            filled[slot] = flat[pl.ds(start, HEIGHT), :]
        span = slice(i * quarter, (i + 1) * quarter)
        out = pltpu.make_async_copy(filled.at[span], out_ref.at[span], sems.at[5 + i])
        out.start()
        outs.append(out)
    for out in outs:
        out.wait()


def rest_kernel(orbital, maps, leaves_ref, out_ref, rows, flat, filled, sems):
    number = 7 * PARENTS
    pairs = []
    for i in range(3):
        span = slice(i * number, (i + 1) * number)
        source = leaves_ref.at[orbital : orbital + COUNT, PER + i * number : PER + (i + 1) * number, :]
        pairs.append((source, rows.at[:, span, :]))
    copies = fetch(pairs, sems)
    outs = []
    for i in range(3):
        copies[i].wait()
        pack_rows(rows, i * number, number, flat)
        for child in range(number):
            filled[i, maps[TAKE + i + 1, PARENTS + child]] = block(flat, i * number + child)
        out = pltpu.make_async_copy(filled.at[i], out_ref.at[i], sems.at[3 + i])
        out.start()
        outs.append(out)
    for out in outs:
        out.wait()


def one_hot(dims, axis, index):
    return (lax.broadcasted_iota(jnp.int32, dims, axis) == index).astype(f32)


def plane_index(dims, axis, size):
    position = lax.broadcasted_iota(jnp.int32, dims, axis)
    w, cell = (position >> 7, position & 127)
    j = (cell * 205) >> 11
    k = cell - DEGREE * j
    if size > DEGREE:
        j, k = (j + DEGREE * (w >> 1), k + DEGREE * (w & 1))
    dead = cell >= PLANE
    return jnp.where(dead, -1, j), jnp.where(dead, -1, k)


def exact(left, right, dims=((1,), (0,))):
    return lax.dot_general(left, right, (dims, ((), ())), precision=highest, preferred_element_type=f32)


def planes(filters, outs, ins):
    rows, columns = ((ins // DEGREE) ** 2 * 128, (outs // DEGREE) ** 2 * 128)
    factors = []
    for left, right in zip(plane_index((rows, ins), 0, ins), plane_index((outs, columns), 1, outs)):
        half = exact(one_hot((rows, ins), 1, left), filters, ((1,), (1,)))
        factors.append(exact(half, one_hot((outs, columns), 0, right)))
    return split(factors[0] * factors[1])


def spread(filters, outs, ins):
    rows, columns = (outs * ROWS, ins * ROWS)
    left = one_hot((rows, outs), 1, lax.broadcasted_iota(jnp.int32, (rows, outs), 0) >> 4)
    right = one_hot((ins, columns), 0, lax.broadcasted_iota(jnp.int32, (ins, columns), 1) >> 4)
    row = lax.broadcasted_iota(jnp.int32, (rows, columns), 0) & (ROWS - 1)
    column = lax.broadcasted_iota(jnp.int32, (rows, columns), 1) & (ROWS - 1)
    return split(jnp.where(row == column, exact(exact(left, filters), right), 0.0))


def weight_kernel(up_ref, down_ref, bank_ref, bank, sem):
    both = exact(down_ref[...], up_ref[...])
    up, down = (up_ref[0:DEGREE, :], down_ref[:, 0:DEGREE])
    sizes = ((up, 10, 20), (both, 20, 20), (down, 20, 10))
    plane_values = [planes(*size) for size in sizes]
    row_values = [spread(*size) for size in sizes]
    for i in range(2):
        bank[PLANE_ROW + 512 * i : PLANE_ROW + 512 * (i + 1), 512:640] = plane_values[0][i]
        bank[PLANE_ROW + 512 * i : PLANE_ROW + 512 * (i + 1), 0:512] = plane_values[1][i]
        bank[DOWN_PLANE + 128 * i : DOWN_PLANE + 128 * (i + 1), 0:512] = plane_values[2][i]
        bank[UP_ROW + 160 * i : UP_ROW + 160 * (i + 1), 0:320] = row_values[0][i]
        bank[BOTH_ROW + 320 * i : BOTH_ROW + 320 * (i + 1), 0:320] = row_values[1][i]
        bank[DOWN_ROW + 320 * i : DOWN_ROW + 320 * (i + 1), 0:160] = row_values[2][i]
    copy = pltpu.make_async_copy(bank, bank_ref.at[0:BANK_USED, :], sem)
    copy.start()
    copy.wait()


def section(bank_ref, start, rows, first, columns):
    return [bank_ref.at[start + i * rows : start + (i + 1) * rows, first : first + columns] for i in range(2)]


def up_weights(bank_ref):
    return section(bank_ref, PLANE_ROW, 512, 512, 128) + section(bank_ref, UP_ROW, 160, 0, 384)


def both_weights(bank_ref):
    return section(bank_ref, PLANE_ROW, 512, 0, 512) + section(bank_ref, BOTH_ROW, 320, 0, 384)


def down_weights(bank_ref):
    return section(bank_ref, DOWN_PLANE, 128, 0, 512) + section(bank_ref, DOWN_ROW, 320, 0, 256)


def split_children(splits_ref, height):
    return section(splits_ref, 2 * WIDE * height, WIDE, 0, 512)


def window_octants(placed, high_ref, low_ref):
    for n in range(COUNT):
        for octant in range(8):
            first = (n * 8 + octant) * 8
            chunks = [placed[(first + part) * ROWS : (first + part + 1) * ROWS, :] for part in range(8)]
            x, w = divmod(octant, 4)
            for i, value in enumerate(windows(chunks)):
                high, low = split(value)
                start = (n * 20 + x * DEGREE + i) * ROWS
                high_ref[start : start + ROWS, w * 128 : w * 128 + 128] = high
                low_ref[start : start + ROWS, w * 128 : w * 128 + 128] = low


def place_children(height, maps, arrived_ref, placed):
    for child in range(PER):
        octant, parent = (child % 8, child // 8)
        slot = maps[PLACE + height, child]
        for n in range(COUNT):
            value = arrived_ref[slot, n * 8 : n * 8 + 8, :]
            placed[pl.ds((n * 8 + octant) * 8 * ROWS + parent, 8, stride=ROWS), :] = value


def filtered(data, weights):
    half = split(product(data, (weights[0][...], weights[1][...])))
    depth = half[0].shape[0] // COUNT
    rows = (weights[2][:, :depth], weights[3][:, :depth])
    return [product(rows, tuple(one[n * depth : (n + 1) * depth] for one in half)) for n in range(COUNT)]


def up_kernel(height, arrived_ref, maps_ref, bank_ref, filled_ref, *rest):
    out_ref, kept_ref, maps, high, low, placed, blocks, v0, v1, v2, v3, sems = rest[-12:]
    weights = (v0, v1, v2, v3)
    pairs = [(maps_ref, maps)] + list(zip(up_weights(bank_ref), weights)) + [(filled_ref.at[height], out_ref)]
    copies = fetch(pairs, sems)
    copies[0].wait()
    place_children(height, maps, arrived_ref, placed)
    window_octants(placed, high, low)
    targets = split_children(kept_ref, height)
    outs = [pltpu.make_async_copy(high, targets[0], sems.at[6]), pltpu.make_async_copy(low, targets[1], sems.at[7])]
    for out in outs:
        out.start()
    for copy in copies[1:5]:
        copy.wait()
    values = filtered((high[...], low[...]), weights)
    for n in range(COUNT):
        parts = [values[n][i * ROWS : (i + 1) * ROWS, :] for i in range(DEGREE)]
        for part, chunk in enumerate(merge(parts)):
            blocks[pl.ds(n * 8 + part, PARENTS, stride=HEIGHT), :] = chunk
    copies[5].wait()
    for child in range(PARENTS):
        out_ref[maps[TAKE + height + 1, child]] = block(blocks, child)
    for out in outs:
        out.wait()


def emit(height, maps, refined, blocks, out_ref):
    for octant in range(8):
        x, w = divmod(octant, 4)
        for n in range(COUNT):
            parts = []
            for i in range(DEGREE):
                start = (n * 20 + x * DEGREE + i) * ROWS
                parts.append(refined[start : start + ROWS, w * 128 : w * 128 + 128])
            for part, value in enumerate(merge(parts)):
                blocks[pl.ds(octant * HEIGHT + n * 8 + part, PARENTS, stride=8 * HEIGHT), :] = value
    for child in range(PER):
        out_ref[maps[PLACE + height, child]] = block(blocks, child)


def keep(refined, values):
    depth = WIDE // COUNT
    for n in range(COUNT):
        refined[n * depth : (n + 1) * depth, :] = values[n]


def top_kernel(height, arrived_ref, maps_ref, bank_ref, out_ref, *scratch):
    maps, high, low, placed, refined, blocks, v0, v1, v2, v3, sems = scratch
    weights = (v0, v1, v2, v3)
    copies = fetch([(maps_ref, maps)] + list(zip(both_weights(bank_ref), weights)), sems)
    copies[0].wait()
    place_children(height, maps, arrived_ref, placed)
    window_octants(placed, high, low)
    for copy in copies[1:]:
        copy.wait()
    keep(refined, filtered((high[...], low[...]), weights))
    emit(height, maps, refined, blocks, out_ref)


def base_kernel(bank_ref, splits_ref, out_ref, *scratch):
    data, weights, refined, sems = (scratch[0:6], scratch[6:18], scratch[18], scratch[19])
    both, up, down = (weights[0:4], weights[4:8], weights[8:12])
    pairs = list(zip(both_weights(bank_ref) + up_weights(bank_ref) + down_weights(bank_ref), weights))
    for height in range(3):
        pairs += list(zip(split_children(splits_ref, height), data[2 * height : 2 * height + 2]))
    copies = fetch(pairs, sems)
    for copy in copies[:12]:
        copy.wait()
    outs = []
    for i in range(3):
        copies[12 + 2 * i].wait()
        copies[13 + 2 * i].wait()
        children = (data[2 * i][...], data[2 * i + 1][...])
        corner = jnp.concatenate(filtered(children, up), axis=0)
        inner = filtered(split(corner), down)
        keep(refined.at[i], [whole - part for whole, part in zip(filtered(children, both), inner)])
        out = pltpu.make_async_copy(refined.at[i], out_ref.at[i], sems.at[18 + i])
        out.start()
        outs.append(out)
    for out in outs:
        out.wait()


def down_kernel(height, returned_ref, maps_ref, base_ref, bank_ref, out_ref, *scratch):
    maps, base, placed, high, low, refined, blocks, v0, v1, v2, v3, sems = scratch
    weights = (v0, v1, v2, v3)
    pairs = [(maps_ref, maps)] + list(zip(down_weights(bank_ref), weights)) + [(base_ref.at[height], base)]
    copies = fetch(pairs, sems)
    copies[0].wait()
    for child in range(PARENTS):
        slot = maps[TAKE + height + 1, child]
        for n in range(COUNT):
            placed[pl.ds(n * 8 * ROWS + child, 8, stride=ROWS), :] = returned_ref[slot, n * 8 : n * 8 + 8, :]
    for n in range(COUNT):
        chunks = [placed[(n * 8 + part) * ROWS : (n * 8 + part + 1) * ROWS, :] for part in range(8)]
        for i, value in enumerate(windows(chunks)):
            start = (n * DEGREE + i) * ROWS
            high[start : start + ROWS, :], low[start : start + ROWS, :] = split(value)
    for copy in copies[1:5]:
        copy.wait()
    values = filtered((high[...], low[...]), weights)
    copies[5].wait()
    depth = WIDE // COUNT
    keep(refined, [base[n * depth : (n + 1) * depth, :] + values[n] for n in range(COUNT)])
    emit(height, maps, refined, blocks, out_ref)


def store_kernel(height, orbital, returned_ref, maps_ref, *rest):
    out_ref, maps, flat, rows, sems = rest[-5:]
    start, number = leaf_range(height)
    skip = PER - number
    copy = fetch([(maps_ref, maps)], sems)[0]
    copy.wait()
    outs = []
    step = 16
    for base in range(0, number, step):
        for child in range(base, base + step):
            flat[child * HEIGHT : (child + 1) * HEIGHT, :] = returned_ref[maps[TAKE + height, child + skip]]
        for first in range(base, base + step, 8):
            for n in range(COUNT):
                for part in range(8):
                    value = flat[pl.ds(first * HEIGHT + n * 8 + part, 8, stride=HEIGHT), :]
                    if part < 7:
                        rows[n, first : first + 8, 128 * part : 128 * part + 128] = value
                    else:
                        rows[n, first : first + 8, 896:CELLS] = value[:, : CELLS - 896]
        span = slice(base, base + step)
        target = out_ref.at[orbital : orbital + COUNT, start + base : start + base + step, :]
        out = pltpu.make_async_copy(rows.at[:, span, :], target, sems.at[1 + base // step])
        out.start()
        outs.append(out)
    for out in outs:
        out.wait()


def shape(*dims, dtype=f32):
    return jax.ShapeDtypeStruct(dims, dtype)


def call(kernel, out_shape, in_specs, out_specs, scratch, operands, flops, name, aliases=None, limit=LIMIT):
    moved = sum(4 * one.size for one in operands)
    return pl.pallas_call(
        kernel,
        out_shape=out_shape,
        in_specs=in_specs,
        out_specs=out_specs,
        scratch_shapes=scratch,
        input_output_aliases=aliases or {},
        compiler_params=pltpu.CompilerParams(vmem_limit_bytes=limit),
        cost_estimate=pl.CostEstimate(flops=flops, bytes_accessed=moved, transcendentals=0),
        name=name,
    )(*operands)


def invert(mapping):
    match = mapping[:, None, :] == jnp.arange(PER, dtype=jnp.int32)[None, :, None]
    return jnp.sum(jnp.where(match, jnp.arange(mapping.shape[1], dtype=jnp.int32)[None, None, :], 0), axis=2)


def exchange(blocks):
    return lax.all_to_all(blocks, "dev", split_axis=0, concat_axis=0, tiled=True)


def flat(number):
    return pltpu.VMEM((number * HEIGHT, 128), f32)


def halves(*dims):
    return [pltpu.VMEM(one, bf16) for one in dims for _ in range(2)]


class Chain:
    def __init__(self, orbital, rows, send_slot):
        self.orbital = orbital
        self.rows = rows
        self.slots = shape(SLOTS, HEIGHT, 128)
        self.placed = pltpu.VMEM((COUNT * 8 * 8 * ROWS, 128), f32)
        self.going = call(
            functools.partial(first_kernel, orbital),
            self.slots,
            [HBM, HBM],
            HBM,
            [pltpu.SMEM(send_slot.shape, jnp.int32), pltpu.VMEM((COUNT, PER, CELLS), f32), flat(PER)]
            + [pltpu.VMEM((SLOTS, HEIGHT, 128), f32), DMA((9,))],
            (send_slot, rows),
            0,
            "pack_first",
            limit=FULL,
        )

    def swap(self):
        self.arrived = exchange(self.going)

    def prepare(self, maps, bank):
        self.maps, self.bank = (maps, bank)
        self.maps_smem = pltpu.SMEM(maps.shape, jnp.int32)
        self.filled = call(
            functools.partial(rest_kernel, self.orbital),
            shape(LEVEL_ROOM, SLOTS, HEIGHT, 128),
            [SMEM, HBM],
            HBM,
            [pltpu.VMEM((COUNT, 336, CELLS), f32), flat(336), pltpu.VMEM((3, SLOTS, HEIGHT, 128), f32), DMA((6,))],
            (maps, self.rows),
            0,
            "pack_rest",
            limit=FULL,
        )
        self.splits = None

    def up(self, height):
        weights = halves((512, 128), (160, 384))
        scratch = [self.maps_smem] + halves((WIDE, 512)) + [self.placed, flat(PARENTS)] + weights + [DMA((8,))]
        operands = (self.arrived, self.maps, self.bank, self.filled)
        aliases = {}
        if self.splits is not None:
            operands += (self.splits,)
            aliases[4] = 1
        self.going, self.splits = call(
            functools.partial(up_kernel, height),
            (self.slots, shape(SPLITS, 512, dtype=bf16)),
            [VMEM] + [HBM] * (len(operands) - 1),
            (VMEM, HBM),
            scratch,
            operands,
            300_000_000,
            "up",
            aliases,
        )

    def base(self):
        self.bases = call(
            base_kernel,
            shape(BASE_ROOM, WIDE, 512),
            [HBM, HBM],
            HBM,
            halves((WIDE, 512)) * 3
            + halves((512, 512), (320, 384), (512, 128), (160, 384), (128, 512), (320, 256))
            + [pltpu.VMEM((3, WIDE, 512), f32), DMA((21,))],
            (self.bank, self.splits),
            3_600_000_000,
            "base",
            limit=FULL,
        )

    def top(self, height):
        scratch = [self.maps_smem] + halves((WIDE, 512)) + [self.placed, pltpu.VMEM((WIDE, 512), f32), flat(PER)]
        scratch += halves((512, 512), (320, 384)) + [DMA((5,))]
        self.going = call(
            functools.partial(top_kernel, height),
            self.slots,
            [VMEM, HBM, HBM],
            VMEM,
            scratch,
            (self.arrived, self.maps, self.bank),
            1_200_000_000,
            "top",
        )

    def down(self, height):
        scratch = [self.maps_smem, pltpu.VMEM((WIDE, 512), f32), pltpu.VMEM((COUNT * 8 * ROWS, 128), f32)]
        scratch += halves((WIDE // 2, 128)) + [pltpu.VMEM((WIDE, 512), f32), flat(PER)]
        scratch += halves((128, 512), (320, 256)) + [DMA((6,))]
        self.going = call(
            functools.partial(down_kernel, height),
            self.slots,
            [VMEM] + [HBM] * 3,
            VMEM,
            scratch,
            (self.arrived, self.maps, self.bases, self.bank),
            400_000_000,
            "down",
        )

    def store(self, height, result):
        start, number = leaf_range(height)
        final = shape(2, PER + 336, CELLS)
        scratch = [self.maps_smem, flat(number), pltpu.VMEM((COUNT, number, CELLS), f32), DMA((1 + number // 16,))]
        kernel = functools.partial(store_kernel, height, self.orbital)
        operands = (self.arrived, self.maps) if result is None else (self.arrived, self.maps, result)
        specs = [VMEM, HBM, HBM][: len(operands)]
        aliases = None if result is None else {2: 0}
        return call(kernel, final, specs, HBM, scratch, operands, 0, "store", aliases)


def transform(leaves, send_slot, recv_slot, filter_up, filter_down):
    levels = send_slot.shape[0]
    rows = jnp.swapaxes(leaves, 1, 2)
    chains = [Chain(group[0], rows, send_slot) for group in GROUPS]
    for chain in chains:
        chain.swap()
    maps = jnp.concatenate([invert(send_slot), invert(recv_slot)], axis=0)
    bank = call(
        weight_kernel,
        shape(BANK, 640, dtype=bf16),
        [VMEM, VMEM],
        HBM,
        [pltpu.VMEM((BANK_USED, 640), bf16), DMA],
        (filter_up, filter_down),
        50_000_000,
        "weights",
        limit=FULL,
    )
    for chain in chains:
        chain.prepare(maps, bank)
    for height in range(levels - 1):
        for chain in chains:
            chain.up(height)
            chain.swap()
    height = levels - 1
    for chain in chains:
        chain.base()
        chain.top(height)
        chain.swap()
    result = None
    while True:
        for chain in chains:
            result = chain.store(height, result)
            if height > 0:
                chain.down(height - 1)
                chain.swap()
        if height == 0:
            break
        height -= 1
    return jnp.swapaxes(result, 1, 2)


def solution(mesh):
    in_specs = (P(None, None, "dev"), P(None, "dev"), P(None, "dev"), P(), P())
    out_specs = P(None, None, "dev")
    return jax.shard_map(transform, mesh=mesh, in_specs=in_specs, out_specs=out_specs, check_vma=False)
```

profile of v0, /device:TPU:1, one launch (start us, length us, event | category | flops | bytes accessed | tf_op | source)
XLA Modules:
  0.0 318.6 jit_solution(10825090418610350016)
XLA Ops:
  0.0 2.7 pack_first.1
  2.7 0.0 copy-start.7
  2.8 11.5 %all-to-all-start = ((f32[256,16,128]{2,1,0:T(8,128)}), f32[256,16,128]{2,1,0:T(8,128)S(1)}, u32[]{:S(2)}, u32[]{:S(2)}) async-start(f32[256,16,128]{2,1,0:T(8,128)} %pack_first.1), calls=%async_computation | async-start | bytes 4194304 | tf_op jit(solution)/shard_map/all_to_all | solution.py:426
  14.3 0.2 select_reduce_fusion
  14.5 0.6 pad_add_fusion.maps.maps_ref
  15.1 4.9 %pack_rest.1.filled_ref = f32[6,256,16,128]{3,2,1,0:T(8,128)} custom-call(s32[8,128]{1,0:T(8,128)} %pad_add_fusion.maps.maps_ref, f32[2,464,1000]{2,1,0:T(8,128)} %bitcast.3), custom_call_target="tpu_custom_call" | custom-call | bytes 3716096 | tf_op jit(solution)/shard_map/pack_rest/pallas_call | solution.py:407
  20.1 8.7 %weights.1.bank_ref = bf16[8448,640]{1,0:T(8,128)(2,1)} custom-call(f32[20,20]{1,0:T(8,128)} %up_ref.1, f32[20,20]{1,0:T(8,128)} %down_ref.1), custom_call_target="tpu_custom_call" | custom-call | flops 50000000 | bytes 3200 | tf_op jit(solution)/shard_map/weights/pallas_call | solution.py:407
  28.8 16.0 %all-to-all-done.arrived_ref = f32[256,16,128]{2,1,0:T(8,128)S(1)} async-done(((f32[256,16,128]{2,1,0:T(8,128)}), f32[256,16,128]{2,1,0:T(8,128)S(1)}, u32[]{:S(2)}, u32[]{:S(2)}) %all-to-all-start) | async-done | bytes 2097184 | tf_op jit(solution)/shard_map/all_to_all | solution.py:426
  44.8 2.8 up.3
  47.7 34.4 %all_to_all.40.arrived_ref = f32[256,16,128]{2,1,0:T(8,128)S(1)} all-to-all(f32[256,16,128]{2,1,0:T(8,128)S(1)} %get-tuple-element.11), channel_id=1, replica_groups=mesh['dev'=128] {'dev'}, dimensions={0} | all-to-all | bytes 4194304 | tf_op jit(solution)/shard_map/all_to_all | solution.py:426
  82.0 2.8 up.4
  84.9 34.6 %all_to_all.41.arrived_ref = f32[256,16,128]{2,1,0:T(8,128)S(1)} all-to-all(f32[256,16,128]{2,1,0:T(8,128)S(1)} %get-tuple-element.13), channel_id=1, replica_groups=mesh['dev'=128] {'dev'}, dimensions={0} | all-to-all | bytes 4194304 | tf_op jit(solution)/shard_map/all_to_all | solution.py:426
  119.5 2.8 up.5
  122.3 34.4 %all_to_all.42.arrived_ref = f32[256,16,128]{2,1,0:T(8,128)S(1)} all-to-all(f32[256,16,128]{2,1,0:T(8,128)S(1)} %get-tuple-element.15), channel_id=1, replica_groups=mesh['dev'=128] {'dev'}, dimensions={0} | all-to-all | bytes 4194304 | tf_op jit(solution)/shard_map/all_to_all | solution.py:426
  156.7 4.4 %top.1 = f32[256,16,128]{2,1,0:T(8,128)S(1)} custom-call(f32[256,16,128]{2,1,0:T(8,128)S(1)} %all_to_all.42.arrived_ref, s32[8,128]{1,0:T(8,128)S(1)} %copy-done.6, bf16[8448,640]{1,0:T(8,128)(2,1)} %weights.1.bank_ref), custom_call_target="tpu_custom_call" | custom-call | flops 1200000000 | bytes 23728128 | tf_op jit(solution)/shard_map/top/pallas_call | solution.py:407
  161.2 1.3 copy-done.4
  162.5 4.4 %all-to-all-start.4 = ((f32[256,16,128]{2,1,0:T(8,128)}), f32[256,16,128]{2,1,0:T(8,128)S(1)}, u32[]{:S(2)}, u32[]{:S(2)}) async-start(f32[256,16,128]{2,1,0:T(8,128)} %copy-done.4), calls=%async_computation.4 | async-start | bytes 4194304 | tf_op jit(solution)/shard_map/all_to_all | solution.py:426
  166.9 17.5 %base.1.base_ref = f32[9,640,512]{2,1,0:T(8,128)} custom-call(bf16[8448,640]{1,0:T(8,128)(2,1)} %weights.1.bank_ref, bf16[10496,512]{1,0:T(8,128)(2,1)} %get-tuple-element.16.splits_ref), custom_call_target="tpu_custom_call" | custom-call | flops 3600000000 | bytes 43122688 | tf_op jit(solution)/shard_map/base/pallas_call | solution.py:407
  184.4 13.1 %all-to-all-done.4.returned_ref = f32[256,16,128]{2,1,0:T(8,128)S(1)} async-done(((f32[256,16,128]{2,1,0:T(8,128)}), f32[256,16,128]{2,1,0:T(8,128)S(1)}, u32[]{:S(2)}, u32[]{:S(2)}) %all-to-all-start.4) | async-done | bytes 2097184 | tf_op jit(solution)/shard_map/all_to_all | solution.py:426
  197.5 3.2 %down.3 = f32[256,16,128]{2,1,0:T(8,128)S(1)} custom-call(f32[256,16,128]{2,1,0:T(8,128)S(1)} %all-to-all-done.4.returned_ref, s32[8,128]{1,0:T(8,128)S(1)} %copy-done.6, f32[9,640,512]{2,1,0:T(8,128)} %base.1.base_ref, bf16[8448,640]{1,0:T(8,128)(2,1)} %weights.1.bank_ref), custom_call_target="tpu_custom_call" | custom-call | flops 400000000 | bytes 35524608 | tf_op jit(solution)/shard_map/down/pallas_call | solution.py:407
  200.7 34.4 %all_to_all.43.returned_ref = f32[256,16,128]{2,1,0:T(8,128)S(1)} all-to-all(f32[256,16,128]{2,1,0:T(8,128)S(1)} %down.3), channel_id=1, replica_groups=mesh['dev'=128] {'dev'}, dimensions={0} | all-to-all | bytes 4194304 | tf_op jit(solution)/shard_map/all_to_all | solution.py:426
  235.1 3.9 %down.4 = f32[256,16,128]{2,1,0:T(8,128)S(1)} custom-call(f32[256,16,128]{2,1,0:T(8,128)S(1)} %all_to_all.43.returned_ref, s32[8,128]{1,0:T(8,128)S(1)} %copy-done.6, f32[9,640,512]{2,1,0:T(8,128)} %base.1.base_ref, bf16[8448,640]{1,0:T(8,128)(2,1)} %weights.1.bank_ref), custom_call_target="tpu_custom_call" | custom-call | flops 400000000 | bytes 35524608 | tf_op jit(solution)/shard_map/down/pallas_call | solution.py:407
  239.1 34.4 %all_to_all.44.returned_ref = f32[256,16,128]{2,1,0:T(8,128)S(1)} all-to-all(f32[256,16,128]{2,1,0:T(8,128)S(1)} %down.4), channel_id=1, replica_groups=mesh['dev'=128] {'dev'}, dimensions={0} | all-to-all | bytes 4194304 | tf_op jit(solution)/shard_map/all_to_all | solution.py:426
  273.4 3.2 %down.5 = f32[256,16,128]{2,1,0:T(8,128)S(1)} custom-call(f32[256,16,128]{2,1,0:T(8,128)S(1)} %all_to_all.44.returned_ref, s32[8,128]{1,0:T(8,128)S(1)} %copy-done.6, f32[9,640,512]{2,1,0:T(8,128)} %base.1.base_ref, bf16[8448,640]{1,0:T(8,128)(2,1)} %weights.1.bank_ref), custom_call_target="tpu_custom_call" | custom-call | flops 400000000 | bytes 35524608 | tf_op jit(solution)/shard_map/down/pallas_call | solution.py:407
  276.7 1.3 copy-done.2
  278.0 1.3 copy-done.5
  279.3 5.4 %all-to-all-start.7 = ((f32[256,16,128]{2,1,0:T(8,128)}), f32[256,16,128]{2,1,0:T(8,128)}, u32[]{:S(2)}, u32[]{:S(2)}) async-start(f32[256,16,128]{2,1,0:T(8,128)} %copy-done.5), calls=%async_computation.7 | async-start | bytes 4194304 | tf_op jit(solution)/shard_map/all_to_all | solution.py:426
  284.8 1.7 store.4.rest_0_
  286.5 1.7 store.5.rest_0_
  288.3 1.7 store.6.rest_0_
  290.1 25.0 %all-to-all-done.7.returned_ref = f32[256,16,128]{2,1,0:T(8,128)} async-done(((f32[256,16,128]{2,1,0:T(8,128)}), f32[256,16,128]{2,1,0:T(8,128)}, u32[]{:S(2)}, u32[]{:S(2)}) %all-to-all-start.7) | async-done | bytes 2097184 | tf_op jit(solution)/shard_map/all_to_all | solution.py:426
  315.1 3.4 %store.7 = f32[2,464,1000]{2,1,0:T(8,128)} custom-call(f32[256,16,128]{2,1,0:T(8,128)} %all-to-all-done.7.returned_ref, s32[8,128]{1,0:T(8,128)S(1)} %copy-done.6, f32[2,464,1000]{2,1,0:T(8,128)} %store.6.rest_0_), custom_call_target="tpu_custom_call", output_to_operand_aliasing={{}: (2, {})} | custom-call | bytes 5813248 | tf_op jit(solution)/shard_map/store/pallas_call | solution.py:407
  (14 shorter events, 0.0 us)
Async XLA Ops:
  2.7 11.5 %copy-start.7 = (s32[4,256]{1,0:T(4,128)S(1)}, s32[4,256]{1,0:T(4,128)}, u32[]{:S(2)}) copy-start(s32[4,256]{1,0:T(4,128)} %send_ref.1) | copy-start | bytes 12292
  2.8 11.5 %copy-start.8 = (s32[4,256]{1,0:T(4,128)S(1)}, s32[4,256]{1,0:T(4,128)}, u32[]{:S(2)}) copy-start(s32[4,256]{1,0:T(4,128)} %param.7) | copy-start | bytes 12292
  2.8 42.0 %all-to-all-start = ((f32[256,16,128]{2,1,0:T(8,128)}), f32[256,16,128]{2,1,0:T(8,128)S(1)}, u32[]{:S(2)}, u32[]{:S(2)}) async-start(f32[256,16,128]{2,1,0:T(8,128)} %pack_first.1), calls=%async_computation | async-start | bytes 4194304 | tf_op jit(solution)/shard_map/all_to_all | solution.py:426
  20.1 24.7 %copy-start.6 = (s32[8,128]{1,0:T(8,128)S(1)}, s32[8,128]{1,0:T(8,128)}, u32[]{:S(2)}) copy-start(s32[8,128]{1,0:T(8,128)} %pad_add_fusion.maps.maps_ref) | copy-start | bytes 12292
  161.2 1.3 copy-start.4
  162.5 35.0 %all-to-all-start.4 = ((f32[256,16,128]{2,1,0:T(8,128)}), f32[256,16,128]{2,1,0:T(8,128)S(1)}, u32[]{:S(2)}, u32[]{:S(2)}) async-start(f32[256,16,128]{2,1,0:T(8,128)} %copy-done.4), calls=%async_computation.4 | async-start | bytes 4194304 | tf_op jit(solution)/shard_map/all_to_all | solution.py:426
  235.1 3.9 %copy-start = (f32[256,16,128]{2,1,0:T(8,128)}, f32[256,16,128]{2,1,0:T(8,128)S(1)}, u32[]{:S(2)}) copy-start(f32[256,16,128]{2,1,0:T(8,128)S(1)} %all_to_all.43.returned_ref) | copy-start | bytes 6291460
  276.7 1.3 copy-start.2
  278.0 1.3 copy-start.5
  279.3 35.8 %all-to-all-start.7 = ((f32[256,16,128]{2,1,0:T(8,128)}), f32[256,16,128]{2,1,0:T(8,128)}, u32[]{:S(2)}, u32[]{:S(2)}) async-start(f32[256,16,128]{2,1,0:T(8,128)} %copy-done.5), calls=%async_computation.7 | async-start | bytes 4194304 | tf_op jit(solution)/shard_map/all_to_all | solution.py:426
  284.8 1.8 copy-start.1
  286.5 1.8 copy-start.3
where the time goes:
time: 319 us
  blocking collectives  172 us (54%)
  Pallas kernels  65.8 us (21%)
  waiting for transfers between devices  54.2 us (17%)
  starting transfers between devices  21.3 us (7%)
  local copies, waits for them, and re-layouts  3.98 us (1%)
    all_to_all x5, blocking collectives, exchange(): lax.all_to_all(blocks, 'dev', split_axis=0, concat_axis=0, tiled=True)  172 us
    pallas_call x15, Pallas kernels, call(): pl.pallas_call(kernel, out_shape=out_shape, in_specs=in_specs, out_specs=...  65.8 us
    all_to_all x3, waiting for transfers between devices, exchange(): lax.all_to_all(blocks, 'dev', split_axis=0, concat_axis=0, tiled=True)  54.2 us
    all_to_all x3, starting transfers between devices, exchange(): lax.all_to_all(blocks, 'dev', split_axis=0, concat_axis=0, tiled=True)  21.3 us
  transfers between devices with their start and end apart: 3, of which 3 were waited for; matrix products, arithmetic and copies ran while one was open for 0% of the time, Pallas kernels for 11%

commit v1 on v0

--- a/solution.py
+++ b/solution.py
@@ -22,8 +22,8 @@
 FULL = 63_400_000
 TAKE = 0
 PLACE = 4
-UP_ROW, BOTH_ROW, DOWN_ROW, PLANE_ROW, DOWN_PLANE, BANK_USED = (0, 320, 960, 1600, 2624, 2880)
-BANK = 8448
+UP_ROW, BOTH_ROW, DOWN_ROW, BOTH_PLANE, UP_PLANE, DOWN_PLANE, BANK_USED = (0, 160, 480, 800, 1312, 1824, 2080)
+BANK = 5376
 SPLITS = 10496
 LEVEL_ROOM = 12 // COUNT
 BASE_ROOM = 18 // COUNT
@@ -48,9 +48,8 @@
     return high, (value - high.astype(f32)).astype(bf16)
 
 
-def product(left, right):
-    dot = functools.partial(jnp.dot, preferred_element_type=f32)
-    return dot(left[0], right[0]) + (dot(left[0], right[1]) + dot(left[1], right[0]))
+def dot(left, right):
+    return jnp.dot(left, right, preferred_element_type=f32)
 
 
 def windows(chunks):
@@ -199,39 +198,74 @@
 def weight_kernel(up_ref, down_ref, bank_ref, bank, sem):
     both = exact(down_ref[...], up_ref[...])
     up, down = (up_ref[0:DEGREE, :], down_ref[:, 0:DEGREE])
-    sizes = ((up, 10, 20), (both, 20, 20), (down, 20, 10))
-    plane_values = [planes(*size) for size in sizes]
-    row_values = [spread(*size) for size in sizes]
-    for i in range(2):
-        bank[PLANE_ROW + 512 * i : PLANE_ROW + 512 * (i + 1), 512:640] = plane_values[0][i]
-        bank[PLANE_ROW + 512 * i : PLANE_ROW + 512 * (i + 1), 0:512] = plane_values[1][i]
-        bank[DOWN_PLANE + 128 * i : DOWN_PLANE + 128 * (i + 1), 0:512] = plane_values[2][i]
-        bank[UP_ROW + 160 * i : UP_ROW + 160 * (i + 1), 0:320] = row_values[0][i]
-        bank[BOTH_ROW + 320 * i : BOTH_ROW + 320 * (i + 1), 0:320] = row_values[1][i]
-        bank[DOWN_ROW + 320 * i : DOWN_ROW + 320 * (i + 1), 0:160] = row_values[2][i]
+    sizes = ((UP_ROW, up, 10, 20), (BOTH_ROW, both, 20, 20), (DOWN_ROW, down, 20, 10))
+    for start, filters, outs, ins in sizes:
+        high, low = spread(filters, outs, ins)
+        rows, depth = (outs * ROWS, ins * ROWS)
+        for i, value in enumerate((high, high, low)):
+            bank[start : start + rows, i * depth : (i + 1) * depth] = value
+    high, low = planes(both, 20, 20)
+    bank[BOTH_PLANE : BOTH_PLANE + 512, 0:512] = high
+    bank[BOTH_PLANE : BOTH_PLANE + 512, 512:1024] = low
+    high, low = planes(up, 10, 20)
+    bank[UP_PLANE : UP_PLANE + 512, 0:128] = high
+    bank[UP_PLANE : UP_PLANE + 512, 128:256] = low
+    high, low = planes(down, 20, 10)
+    bank[DOWN_PLANE : DOWN_PLANE + 128, 0:512] = high
+    bank[DOWN_PLANE + 128 : DOWN_PLANE + 256, 0:512] = high
+    bank[DOWN_PLANE : DOWN_PLANE + 128, 512:1024] = low
     copy = pltpu.make_async_copy(bank, bank_ref.at[0:BANK_USED, :], sem)
     copy.start()
     copy.wait()
 
 
-def section(bank_ref, start, rows, first, columns):
-    return [bank_ref.at[start + i * rows : start + (i + 1) * rows, first : first + columns] for i in range(2)]
+def section(ref, start, rows, columns):
+    return ref.at[start : start + rows, 0:columns]
 
 
 def up_weights(bank_ref):
-    return section(bank_ref, PLANE_ROW, 512, 512, 128) + section(bank_ref, UP_ROW, 160, 0, 384)
+    return [section(bank_ref, UP_PLANE, 512, 256), section(bank_ref, UP_ROW, 160, 1024)]
 
 
 def both_weights(bank_ref):
-    return section(bank_ref, PLANE_ROW, 512, 0, 512) + section(bank_ref, BOTH_ROW, 320, 0, 384)
+    return [section(bank_ref, BOTH_PLANE, 512, 1024), section(bank_ref, BOTH_ROW, 320, 1024)]
 
 
 def down_weights(bank_ref):
-    return section(bank_ref, DOWN_PLANE, 128, 0, 512) + section(bank_ref, DOWN_ROW, 320, 0, 256)
+    return [section(bank_ref, DOWN_PLANE, 256, 1024), section(bank_ref, DOWN_ROW, 320, 512)]
+
+
+def stacked(value):
+    high, low = split(value)
+    return jnp.concatenate([high, low, high], axis=0)
+
+
+def up_product(high, low, weights):
+    plane, rows = weights
+    wide = dot(high, plane[...])
+    half = wide[:, 0:128] + (wide[:, 128:256] + dot(low, plane[:, 0:128]))
+    depth = 20 * ROWS
+    half = jnp.concatenate([half[n * depth : (n + 1) * depth] for n in range(COUNT)], axis=1)
+    value = dot(rows[:, 0 : 3 * depth], stacked(half))
+    return [value[:, n * 128 : (n + 1) * 128] for n in range(COUNT)]
+
+
+def both_product(high, low, weights):
+    plane, rows = weights
+    half = dot(high, plane[:, 0:512]) + (dot(high, plane[:, 512:1024]) + dot(low, plane[:, 0:512]))
+    depth = 20 * ROWS
+    return [dot(rows[:, 0 : 3 * depth], stacked(half[n * depth : (n + 1) * depth])) for n in range(COUNT)]
+
+
+def down_product(high, low, weights):
+    plane, rows = weights
+    half = dot(jnp.concatenate([high, low], axis=1), plane[:, 0:512]) + dot(high, plane[0:128, 512:1024])
+    depth = DEGREE * ROWS
+    return [dot(rows[:, 0 : 3 * depth], stacked(half[n * depth : (n + 1) * depth])) for n in range(COUNT)]
 
 
 def split_children(splits_ref, height):
-    return section(splits_ref, 2 * WIDE * height, WIDE, 0, 512)
+    return [section(splits_ref, (2 * height + i) * WIDE, WIDE, 512) for i in range(2)]
 
 
 def window_octants(placed, high_ref, low_ref):
@@ -256,33 +290,26 @@
             placed[pl.ds((n * 8 + octant) * 8 * ROWS + parent, 8, stride=ROWS), :] = value
 
 
-def filtered(data, weights):
-    half = split(product(data, (weights[0][...], weights[1][...])))
-    depth = half[0].shape[0] // COUNT
-    rows = (weights[2][:, :depth], weights[3][:, :depth])
-    return [product(rows, tuple(one[n * depth : (n + 1) * depth] for one in half)) for n in range(COUNT)]
-
-
 def up_kernel(height, arrived_ref, maps_ref, bank_ref, filled_ref, *rest):
-    out_ref, kept_ref, maps, high, low, placed, blocks, v0, v1, v2, v3, sems = rest[-12:]
-    weights = (v0, v1, v2, v3)
+    out_ref, kept_ref, maps, high, low, placed, blocks, v0, v1, sems = rest[-10:]
+    weights = (v0, v1)
     pairs = [(maps_ref, maps)] + list(zip(up_weights(bank_ref), weights)) + [(filled_ref.at[height], out_ref)]
     copies = fetch(pairs, sems)
     copies[0].wait()
     place_children(height, maps, arrived_ref, placed)
     window_octants(placed, high, low)
     targets = split_children(kept_ref, height)
-    outs = [pltpu.make_async_copy(high, targets[0], sems.at[6]), pltpu.make_async_copy(low, targets[1], sems.at[7])]
+    outs = [pltpu.make_async_copy(high, targets[0], sems.at[4]), pltpu.make_async_copy(low, targets[1], sems.at[5])]
     for out in outs:
         out.start()
-    for copy in copies[1:5]:
+    for copy in copies[1:3]:
         copy.wait()
-    values = filtered((high[...], low[...]), weights)
+    values = up_product(high[...], low[...], weights)
     for n in range(COUNT):
         parts = [values[n][i * ROWS : (i + 1) * ROWS, :] for i in range(DEGREE)]
         for part, chunk in enumerate(merge(parts)):
             blocks[pl.ds(n * 8 + part, PARENTS, stride=HEIGHT), :] = chunk
-    copies[5].wait()
+    copies[3].wait()
     for child in range(PARENTS):
         out_ref[maps[TAKE + height + 1, child]] = block(blocks, child)
     for out in outs:
@@ -310,45 +337,59 @@
 
 
 def top_kernel(height, arrived_ref, maps_ref, bank_ref, out_ref, *scratch):
-    maps, high, low, placed, refined, blocks, v0, v1, v2, v3, sems = scratch
-    weights = (v0, v1, v2, v3)
+    maps, high, low, placed, refined, blocks, v0, v1, sems = scratch
+    weights = (v0, v1)
     copies = fetch([(maps_ref, maps)] + list(zip(both_weights(bank_ref), weights)), sems)
     copies[0].wait()
     place_children(height, maps, arrived_ref, placed)
     window_octants(placed, high, low)
     for copy in copies[1:]:
         copy.wait()
-    keep(refined, filtered((high[...], low[...]), weights))
+    keep(refined, both_product(high[...], low[...], weights))
     emit(height, maps, refined, blocks, out_ref)
 
 
 def base_kernel(bank_ref, splits_ref, out_ref, *scratch):
-    data, weights, refined, sems = (scratch[0:6], scratch[6:18], scratch[18], scratch[19])
-    both, up, down = (weights[0:4], weights[4:8], weights[8:12])
+    data, weights, refined, sems = (scratch[0:6], scratch[6:12], scratch[12], scratch[13])
+    both, up, down = (weights[0:2], weights[2:4], weights[4:6])
     pairs = list(zip(both_weights(bank_ref) + up_weights(bank_ref) + down_weights(bank_ref), weights))
     for height in range(3):
         pairs += list(zip(split_children(splits_ref, height), data[2 * height : 2 * height + 2]))
     copies = fetch(pairs, sems)
-    for copy in copies[:12]:
+    for copy in copies[:6]:
         copy.wait()
     outs = []
     for i in range(3):
-        copies[12 + 2 * i].wait()
-        copies[13 + 2 * i].wait()
-        children = (data[2 * i][...], data[2 * i + 1][...])
-        corner = jnp.concatenate(filtered(children, up), axis=0)
-        inner = filtered(split(corner), down)
-        keep(refined.at[i], [whole - part for whole, part in zip(filtered(children, both), inner)])
-        out = pltpu.make_async_copy(refined.at[i], out_ref.at[i], sems.at[18 + i])
+        copies[6 + 2 * i].wait()
+        copies[7 + 2 * i].wait()
+        high, low = (data[2 * i][...], data[2 * i + 1][...])
+        corner = jnp.concatenate(up_product(high, low, up), axis=0)
+        inner = down_product(*split(corner), down)
+        keep(refined.at[i], [whole - part for whole, part in zip(both_product(high, low, both), inner)])
+        out = pltpu.make_async_copy(refined.at[i], out_ref.at[i], sems.at[12 + i])
         out.start()
         outs.append(out)
     for out in outs:
         out.wait()
 
 
-def down_kernel(height, returned_ref, maps_ref, base_ref, bank_ref, out_ref, *scratch):
-    maps, base, placed, high, low, refined, blocks, v0, v1, v2, v3, sems = scratch
-    weights = (v0, v1, v2, v3)
+def gather_leaves(height, first, maps, returned_ref, flat, rows, number):
+    skip = PER - leaf_range(height)[1]
+    for child in range(first, first + number):
+        flat[child * HEIGHT : (child + 1) * HEIGHT, :] = returned_ref[maps[TAKE + height, child + skip]]
+    for start in range(first, first + number, 8):
+        for n in range(COUNT):
+            for part in range(8):
+                value = flat[pl.ds(start * HEIGHT + n * 8 + part, 8, stride=HEIGHT), :]
+                if part < 7:
+                    rows[n, start : start + 8, 128 * part : 128 * part + 128] = value
+                else:
+                    rows[n, start : start + 8, 896:CELLS] = value[:, : CELLS - 896]
+
+
+def down_kernel(height, returned_ref, maps_ref, base_ref, bank_ref, *rest):
+    out_ref, result_ref, maps, base, placed, high, low, refined, blocks, flat_leaves, rows, v0, v1, sems = rest[-14:]
+    weights = (v0, v1)
     pairs = [(maps_ref, maps)] + list(zip(down_weights(bank_ref), weights)) + [(base_ref.at[height], base)]
     copies = fetch(pairs, sems)
     copies[0].wait()
@@ -361,37 +402,29 @@
         for i, value in enumerate(windows(chunks)):
             start = (n * DEGREE + i) * ROWS
             high[start : start + ROWS, :], low[start : start + ROWS, :] = split(value)
-    for copy in copies[1:5]:
+    start, number = leaf_range(height + 1)
+    gather_leaves(height + 1, 0, maps, returned_ref, flat_leaves, rows, number)
+    store = pltpu.make_async_copy(rows, result_ref.at[:, start : start + number, :], sems.at[4])
+    store.start()
+    for copy in copies[1:3]:
         copy.wait()
-    values = filtered((high[...], low[...]), weights)
-    copies[5].wait()
+    values = down_product(high[...], low[...], weights)
+    copies[3].wait()
     depth = WIDE // COUNT
     keep(refined, [base[n * depth : (n + 1) * depth, :] + values[n] for n in range(COUNT)])
     emit(height, maps, refined, blocks, out_ref)
-
-
-def store_kernel(height, orbital, returned_ref, maps_ref, *rest):
-    out_ref, maps, flat, rows, sems = rest[-5:]
-    start, number = leaf_range(height)
-    skip = PER - number
+    store.wait()
+
+
+def store_kernel(returned_ref, maps_ref, _, out_ref, maps, flat, rows, sems):
     copy = fetch([(maps_ref, maps)], sems)[0]
     copy.wait()
     outs = []
-    step = 16
-    for base in range(0, number, step):
-        for child in range(base, base + step):
-            flat[child * HEIGHT : (child + 1) * HEIGHT, :] = returned_ref[maps[TAKE + height, child + skip]]
-        for first in range(base, base + step, 8):
-            for n in range(COUNT):
-                for part in range(8):
-                    value = flat[pl.ds(first * HEIGHT + n * 8 + part, 8, stride=HEIGHT), :]
-                    if part < 7:
-                        rows[n, first : first + 8, 128 * part : 128 * part + 128] = value
-                    else:
-                        rows[n, first : first + 8, 896:CELLS] = value[:, : CELLS - 896]
-        span = slice(base, base + step)
-        target = out_ref.at[orbital : orbital + COUNT, start + base : start + base + step, :]
-        out = pltpu.make_async_copy(rows.at[:, span, :], target, sems.at[1 + base // step])
+    step = 32
+    for first in range(0, PER, step):
+        gather_leaves(0, first, maps, returned_ref, flat, rows, step)
+        span = slice(first, first + step)
+        out = pltpu.make_async_copy(rows.at[:, span, :], out_ref.at[:, span, :], sems.at[1 + first // step])
         out.start()
         outs.append(out)
     for out in outs:
@@ -432,6 +465,10 @@
 
 def halves(*dims):
     return [pltpu.VMEM(one, bf16) for one in dims for _ in range(2)]
+
+
+def single(*dims):
+    return [pltpu.VMEM(one, bf16) for one in dims]
 
 
 class Chain:
@@ -473,8 +510,8 @@
         self.splits = None
 
     def up(self, height):
-        weights = halves((512, 128), (160, 384))
-        scratch = [self.maps_smem] + halves((WIDE, 512)) + [self.placed, flat(PARENTS)] + weights + [DMA((8,))]
+        weights = single((512, 256), (160, 1024))
+        scratch = [self.maps_smem] + halves((WIDE, 512)) + [self.placed, flat(PARENTS)] + weights + [DMA((6,))]
         operands = (self.arrived, self.maps, self.bank, self.filled)
         aliases = {}
         if self.splits is not None:
@@ -499,8 +536,8 @@
             [HBM, HBM],
             HBM,
             halves((WIDE, 512)) * 3
-            + halves((512, 512), (320, 384), (512, 128), (160, 384), (128, 512), (320, 256))
-            + [pltpu.VMEM((3, WIDE, 512), f32), DMA((21,))],
+            + single((512, 1024), (320, 1024), (512, 256), (160, 1024), (256, 1024), (320, 512))
+            + [pltpu.VMEM((3, WIDE, 512), f32), DMA((15,))],
             (self.bank, self.splits),
             3_600_000_000,
             "base",
@@ -509,7 +546,7 @@
 
     def top(self, height):
         scratch = [self.maps_smem] + halves((WIDE, 512)) + [self.placed, pltpu.VMEM((WIDE, 512), f32), flat(PER)]
-        scratch += halves((512, 512), (320, 384)) + [DMA((5,))]
+        scratch += single((512, 1024), (320, 1024)) + [DMA((3,))]
         self.going = call(
             functools.partial(top_kernel, height),
             self.slots,
@@ -521,30 +558,40 @@
             "top",
         )
 
-    def down(self, height):
+    def down(self, height, result):
+        number = leaf_range(height + 1)[1]
         scratch = [self.maps_smem, pltpu.VMEM((WIDE, 512), f32), pltpu.VMEM((COUNT * 8 * ROWS, 128), f32)]
         scratch += halves((WIDE // 2, 128)) + [pltpu.VMEM((WIDE, 512), f32), flat(PER)]
-        scratch += halves((128, 512), (320, 256)) + [DMA((6,))]
-        self.going = call(
+        scratch += [flat(number), pltpu.VMEM((COUNT, number, CELLS), f32)]
+        scratch += single((256, 1024), (320, 512)) + [DMA((5,))]
+        operands = (self.arrived, self.maps, self.bases, self.bank)
+        if result is not None:
+            operands += (result,)
+        self.going, result = call(
             functools.partial(down_kernel, height),
-            self.slots,
-            [VMEM] + [HBM] * 3,
-            VMEM,
+            (self.slots, shape(2, PER + 336, CELLS)),
+            [VMEM] + [HBM] * (len(operands) - 1),
+            (VMEM, HBM),
             scratch,
-            (self.arrived, self.maps, self.bases, self.bank),
+            operands,
             400_000_000,
             "down",
+            None if result is None else {4: 1},
         )
-
-    def store(self, height, result):
-        start, number = leaf_range(height)
-        final = shape(2, PER + 336, CELLS)
-        scratch = [self.maps_smem, flat(number), pltpu.VMEM((COUNT, number, CELLS), f32), DMA((1 + number // 16,))]
-        kernel = functools.partial(store_kernel, height, self.orbital)
-        operands = (self.arrived, self.maps) if result is None else (self.arrived, self.maps, result)
-        specs = [VMEM, HBM, HBM][: len(operands)]
-        aliases = None if result is None else {2: 0}
-        return call(kernel, final, specs, HBM, scratch, operands, 0, "store", aliases)
+        return result
+
+    def store(self, result):
+        return call(
+            store_kernel,
+            shape(*result.shape),
+            [VMEM, HBM, HBM],
+            HBM,
+            [self.maps_smem, flat(PER), pltpu.VMEM((COUNT, PER, CELLS), f32), DMA((5,))],
+            (self.arrived, self.maps, result),
+            0,
+            "store",
+            {2: 0},
+        )
 
 
 def transform(leaves, send_slot, recv_slot, filter_up, filter_down):
@@ -556,10 +603,10 @@
     maps = jnp.concatenate([invert(send_slot), invert(recv_slot)], axis=0)
     bank = call(
         weight_kernel,
-        shape(BANK, 640, dtype=bf16),
+        shape(BANK, 1024, dtype=bf16),
         [VMEM, VMEM],
         HBM,
-        [pltpu.VMEM((BANK_USED, 640), bf16), DMA],
+        [pltpu.VMEM((BANK_USED, 1024), bf16), DMA],
         (filter_up, filter_down),
         50_000_000,
         "weights",
@@ -577,15 +624,12 @@
         chain.top(height)
         chain.swap()
     result = None
-    while True:
+    for height in reversed(range(levels - 1)):
         for chain in chains:
-            result = chain.store(height, result)
-            if height > 0:
-                chain.down(height - 1)
-                chain.swap()
-        if height == 0:
-            break
-        height -= 1
+            result = chain.down(height, result)
+            chain.swap()
+    for chain in chains:
+        result = chain.store(result)
     return jnp.swapaxes(result, 1, 2)
 
 

time: 319 us -> 311 us (0.975)
  blocking collectives: 172 us -> 206 us
  waiting for transfers between devices: 54.2 us -> 33.2 us
  Pallas kernels: 65.8 us -> 52.1 us
  starting transfers between devices: 21.3 us -> 15.9 us
    all_to_all x5 -> x6, blocking collectives: 172 us -> 206 us  [exchange(): lax.all_to_all(blocks, 'dev', split_axis=0, concat_axis=0, tiled=True)]
    all_to_all x3 -> x2, waiting for transfers between devices: 54.2 us -> 33.2 us  [exchange(): lax.all_to_all(blocks, 'dev', split_axis=0, concat_axis=0, tiled=True)]
    pallas_call x15 -> x12, Pallas kernels: 65.8 us -> 52.1 us  [call(): pl.pallas_call(kernel, out_shape=out_shape, in_specs=in_specs, out_specs=...]
    all_to_all x3 -> x2, starting transfers between devices: 21.3 us -> 15.9 us  [exchange(): lax.all_to_all(blocks, 'dev', split_axis=0, concat_axis=0, tiled=True)]
  transfers between devices with their start and end apart: 3 -> 2, of which waited for: 3 -> 2; matrix products, arithmetic and copies ran while one was open for 0% -> 0% of each run, Pallas kernels for 11% -> 9%
where the time goes in v1:
time: 311 us; the launch traced here: 310 us
  blocking collectives  206 us (66%)
  Pallas kernels  52.1 us (17%)
  waiting for transfers between devices  33.2 us (11%)
  starting transfers between devices  15.9 us (5%)
    all_to_all x6, blocking collectives, exchange(): lax.all_to_all(blocks, 'dev', split_axis=0, concat_axis=0, tiled=True)  206 us
    pallas_call x12, Pallas kernels, call(): pl.pallas_call(kernel, out_shape=out_shape, in_specs=in_specs, out_specs=...  52.1 us
    all_to_all x2, waiting for transfers between devices, exchange(): lax.all_to_all(blocks, 'dev', split_axis=0, concat_axis=0, tiled=True)  33.2 us
    all_to_all x2, starting transfers between devices, exchange(): lax.all_to_all(blocks, 'dev', split_axis=0, concat_axis=0, tiled=True)  15.9 us
  transfers between devices with their start and end apart: 2, of which 2 were waited for; matrix products, arithmetic and copies ran while one was open for 0% of the time, Pallas kernels for 9%

profile of v1, /device:TPU:1, one launch (start us, length us, event | category | flops | bytes accessed | tf_op | source)
XLA Modules:
  0.0 310.0 jit_solution(4789371057315435530)
XLA Ops:
  0.0 2.7 pack_first.1
  2.7 0.0 copy-start.2
  2.8 0.0 copy-start.3
  2.8 11.5 %all-to-all-start = ((f32[256,16,128]{2,1,0:T(8,128)}), f32[256,16,128]{2,1,0:T(8,128)S(1)}, u32[]{:S(2)}, u32[]{:S(2)}) async-start(f32[256,16,128]{2,1,0:T(8,128)} %pack_first.1), calls=%async_computation | async-start | bytes 4194304 | tf_op jit(solution)/shard_map/all_to_all | solution.py:459
  14.3 0.0 copy-done.2
  14.3 0.0 copy-done.3
  14.3 0.2 select_reduce_fusion
  14.5 0.6 pad_add_fusion.maps.maps_ref
  15.1 5.0 %pack_rest.1.filled_ref = f32[6,256,16,128]{3,2,1,0:T(8,128)} custom-call(s32[8,128]{1,0:T(8,128)} %pad_add_fusion.maps.maps_ref, f32[2,464,1000]{2,1,0:T(8,128)} %bitcast.3), custom_call_target="tpu_custom_call" | custom-call | bytes 3716096 | tf_op jit(solution)/shard_map/pack_rest/pallas_call | solution.py:440
  20.1 0.0 copy-start.1
  20.1 8.5 %weights.1.bank_ref = bf16[5376,1024]{1,0:T(8,128)(2,1)} custom-call(f32[20,20]{1,0:T(8,128)} %up_ref.1, f32[20,20]{1,0:T(8,128)} %down_ref.1), custom_call_target="tpu_custom_call" | custom-call | flops 50000000 | bytes 3200 | tf_op jit(solution)/shard_map/weights/pallas_call | solution.py:440
  28.7 16.1 %all-to-all-done.arrived_ref = f32[256,16,128]{2,1,0:T(8,128)S(1)} async-done(((f32[256,16,128]{2,1,0:T(8,128)}), f32[256,16,128]{2,1,0:T(8,128)S(1)}, u32[]{:S(2)}, u32[]{:S(2)}) %all-to-all-start) | async-done | bytes 2097184 | tf_op jit(solution)/shard_map/all_to_all | solution.py:459
  44.8 0.0 copy-done.1
  44.8 2.4 up.3
  47.3 34.4 %all_to_all.40.arrived_ref = f32[256,16,128]{2,1,0:T(8,128)S(1)} all-to-all(f32[256,16,128]{2,1,0:T(8,128)S(1)} %get-tuple-element.17), channel_id=1, replica_groups=mesh['dev'=128] {'dev'}, dimensions={0} | all-to-all | bytes 4194304 | tf_op jit(solution)/shard_map/all_to_all | solution.py:459
  81.6 2.5 up.4
  84.2 34.4 %all_to_all.41.arrived_ref = f32[256,16,128]{2,1,0:T(8,128)S(1)} all-to-all(f32[256,16,128]{2,1,0:T(8,128)S(1)} %get-tuple-element.19), channel_id=1, replica_groups=mesh['dev'=128] {'dev'}, dimensions={0} | all-to-all | bytes 4194304 | tf_op jit(solution)/shard_map/all_to_all | solution.py:459
  118.6 2.4 up.5
  121.0 34.4 %all_to_all.42.arrived_ref = f32[256,16,128]{2,1,0:T(8,128)S(1)} all-to-all(f32[256,16,128]{2,1,0:T(8,128)S(1)} %get-tuple-element.21), channel_id=1, replica_groups=mesh['dev'=128] {'dev'}, dimensions={0} | all-to-all | bytes 4194304 | tf_op jit(solution)/shard_map/all_to_all | solution.py:459
  155.4 4.2 %top.1 = f32[256,16,128]{2,1,0:T(8,128)S(1)} custom-call(f32[256,16,128]{2,1,0:T(8,128)S(1)} %all_to_all.42.arrived_ref, s32[8,128]{1,0:T(8,128)S(1)} %copy-done.1, bf16[5376,1024]{1,0:T(8,128)(2,1)} %weights.1.bank_ref), custom_call_target="tpu_custom_call" | custom-call | flops 1200000000 | bytes 24121344 | tf_op jit(solution)/shard_map/top/pallas_call | solution.py:440
  159.6 0.0 copy-start
  159.6 1.3 copy-done
  160.9 4.4 %all-to-all-start.4 = ((f32[256,16,128]{2,1,0:T(8,128)}), f32[256,16,128]{2,1,0:T(8,128)S(1)}, u32[]{:S(2)}, u32[]{:S(2)}) async-start(f32[256,16,128]{2,1,0:T(8,128)} %copy-done), calls=%async_computation.4 | async-start | bytes 4194304 | tf_op jit(solution)/shard_map/all_to_all | solution.py:459
  165.3 13.5 %base.1.base_ref = f32[9,640,512]{2,1,0:T(8,128)} custom-call(bf16[5376,1024]{1,0:T(8,128)(2,1)} %weights.1.bank_ref, bf16[10496,512]{1,0:T(8,128)(2,1)} %get-tuple-element.22.splits_ref), custom_call_target="tpu_custom_call" | custom-call | flops 3600000000 | bytes 43515904 | tf_op jit(solution)/shard_map/base/pallas_call | solution.py:440
  178.8 17.1 %all-to-all-done.4.returned_ref = f32[256,16,128]{2,1,0:T(8,128)S(1)} async-done(((f32[256,16,128]{2,1,0:T(8,128)}), f32[256,16,128]{2,1,0:T(8,128)S(1)}, u32[]{:S(2)}, u32[]{:S(2)}) %all-to-all-start.4) | async-done | bytes 2097184 | tf_op jit(solution)/shard_map/all_to_all | solution.py:459
  195.9 3.0 down.3
  198.9 34.4 %all_to_all.43.returned_ref = f32[256,16,128]{2,1,0:T(8,128)S(1)} all-to-all(f32[256,16,128]{2,1,0:T(8,128)S(1)} %get-tuple-element.23), channel_id=1, replica_groups=mesh['dev'=128] {'dev'}, dimensions={0} | all-to-all | bytes 4194304 | tf_op jit(solution)/shard_map/all_to_all | solution.py:459
  233.3 3.0 down.4
  236.3 34.4 %all_to_all.44.returned_ref = f32[256,16,128]{2,1,0:T(8,128)S(1)} all-to-all(f32[256,16,128]{2,1,0:T(8,128)S(1)} %get-tuple-element.25), channel_id=1, replica_groups=mesh['dev'=128] {'dev'}, dimensions={0} | all-to-all | bytes 4194304 | tf_op jit(solution)/shard_map/all_to_all | solution.py:459
  270.7 3.0 down.5
  273.6 34.4 %all_to_all.45.returned_ref = f32[256,16,128]{2,1,0:T(8,128)S(1)} all-to-all(f32[256,16,128]{2,1,0:T(8,128)S(1)} %get-tuple-element.27), channel_id=1, replica_groups=mesh['dev'=128] {'dev'}, dimensions={0} | all-to-all | bytes 4194304 | tf_op jit(solution)/shard_map/all_to_all | solution.py:459
  308.0 1.8 store.1
Async XLA Ops:
  2.7 11.5 %copy-start.2 = (s32[4,256]{1,0:T(4,128)S(1)}, s32[4,256]{1,0:T(4,128)}, u32[]{:S(2)}) copy-start(s32[4,256]{1,0:T(4,128)} %send_ref.1) | copy-start | bytes 12292
  2.8 11.5 %copy-start.3 = (s32[4,256]{1,0:T(4,128)S(1)}, s32[4,256]{1,0:T(4,128)}, u32[]{:S(2)}) copy-start(s32[4,256]{1,0:T(4,128)} %param.7) | copy-start | bytes 12292
  2.8 42.0 %all-to-all-start = ((f32[256,16,128]{2,1,0:T(8,128)}), f32[256,16,128]{2,1,0:T(8,128)S(1)}, u32[]{:S(2)}, u32[]{:S(2)}) async-start(f32[256,16,128]{2,1,0:T(8,128)} %pack_first.1), calls=%async_computation | async-start | bytes 4194304 | tf_op jit(solution)/shard_map/all_to_all | solution.py:459
  20.1 24.7 %copy-start.1 = (s32[8,128]{1,0:T(8,128)S(1)}, s32[8,128]{1,0:T(8,128)}, u32[]{:S(2)}) copy-start(s32[8,128]{1,0:T(8,128)} %pad_add_fusion.maps.maps_ref) | copy-start | bytes 12292
  159.6 1.3 copy-start
  160.9 35.0 %all-to-all-start.4 = ((f32[256,16,128]{2,1,0:T(8,128)}), f32[256,16,128]{2,1,0:T(8,128)S(1)}, u32[]{:S(2)}, u32[]{:S(2)}) async-start(f32[256,16,128]{2,1,0:T(8,128)} %copy-done), calls=%async_computation.4 | async-start | bytes 4194304 | tf_op jit(solution)/shard_map/all_to_all | solution.py:459

commit v2 on v1

--- a/solution.py
+++ b/solution.py
@@ -2,6 +2,7 @@
 
 import jax
 import jax.numpy as jnp
+import numpy as np
 from jax import lax
 from jax.experimental import pallas as pl
 from jax.experimental.pallas import tpu as pltpu
@@ -13,6 +14,10 @@
 CELLS = 1000
 PLANE = 100
 SLOTS = 256
+DEVICES = 128
+ORDER = [59 * position % DEVICES for position in range(DEVICES)]
+SLOT_ORDER = [2 * device + r for device in ORDER for r in range(2)]
+POSITION = np.argsort(SLOT_ORDER).astype(np.int32)
 GROUPS = ((0, 1),)
 COUNT = len(GROUPS[0])
 HEIGHT = 8 * COUNT
@@ -127,7 +132,7 @@
     quarter = SLOTS // 4
     for i in range(4):
         for slot in range(i * quarter, (i + 1) * quarter):
-            start = pl.multiple_of(jnp.minimum(send[0, slot], PER - 1) * HEIGHT, HEIGHT)
+            start = pl.multiple_of(jnp.minimum(send[0, SLOT_ORDER[slot]], PER - 1) * HEIGHT, HEIGHT)
             filled[slot] = flat[pl.ds(start, HEIGHT), :]
         span = slice(i * quarter, (i + 1) * quarter)
         out = pltpu.make_async_copy(filled.at[span], out_ref.at[span], sems.at[5 + i])
@@ -452,11 +457,13 @@
 
 def invert(mapping):
     match = mapping[:, None, :] == jnp.arange(PER, dtype=jnp.int32)[None, :, None]
-    return jnp.sum(jnp.where(match, jnp.arange(mapping.shape[1], dtype=jnp.int32)[None, None, :], 0), axis=2)
+    return jnp.sum(jnp.where(match, POSITION[None, None, :], 0), axis=2)
 
 
 def exchange(blocks):
-    return lax.all_to_all(blocks, "dev", split_axis=0, concat_axis=0, tiled=True)
+    if lax.axis_size("dev") == 1:
+        return blocks
+    return lax.all_to_all(blocks, "dev", split_axis=0, concat_axis=0, axis_index_groups=[ORDER], tiled=True)
 
 
 def flat(number):

time: 311 us -> 330 us (1.061)
  blocking collectives: 206 us -> 223 us
    all_to_all x6, blocking collectives: 206 us -> 223 us  [exchange(): lax.all_to_all(blocks, 'dev', split_axis=0, concat_axis=0, axis_index_gro...]
  transfers between devices with their start and end apart: 2 -> 2, of which waited for: 2 -> 2; matrix products, arithmetic and copies ran while one was open for 0% -> 0% of each run, Pallas kernels for 9% -> 8%
where the time goes in v2:
time: 330 us; the launch traced here: 329 us
  blocking collectives  223 us (68%)
  Pallas kernels  52.1 us (16%)
  waiting for transfers between devices  33.2 us (10%)
  starting transfers between devices  18.3 us (6%)
    all_to_all x6, blocking collectives, exchange(): lax.all_to_all(blocks, 'dev', split_axis=0, concat_axis=0, axis_index_gro...  223 us
    pallas_call x12, Pallas kernels, call(): pl.pallas_call(kernel, out_shape=out_shape, in_specs=in_specs, out_specs=...  52.1 us
    all_to_all x2, waiting for transfers between devices, exchange(): lax.all_to_all(blocks, 'dev', split_axis=0, concat_axis=0, axis_index_gro...  33.2 us
    all_to_all x2, starting transfers between devices, exchange(): lax.all_to_all(blocks, 'dev', split_axis=0, concat_axis=0, axis_index_gro...  18.3 us
  transfers between devices with their start and end apart: 2, of which 2 were waited for; matrix products, arithmetic and copies ran while one was open for 0% of the time, Pallas kernels for 8%

profile of v2, /device:TPU:1, one launch (start us, length us, event | category | flops | bytes accessed | tf_op | source)
XLA Modules:
  0.0 329.0 jit_solution(16705459252272926747)
XLA Ops:
  0.0 2.7 pack_first.1
  2.7 0.0 copy-start.2
  2.8 0.0 copy-start.3
  2.8 0.0 copy-start.4
  2.8 11.5 %all-to-all-start = ((f32[256,16,128]{2,1,0:T(8,128)}), f32[256,16,128]{2,1,0:T(8,128)S(1)}, u32[]{:S(2)}, u32[]{:S(2)}) async-start(f32[256,16,128]{2,1,0:T(8,128)} %pack_first.1), calls=%async_computation | async-start | bytes 4194304 | tf_op jit(solution)/shard_map/all_to_all | solution.py:466
  14.3 0.0 copy-done.2
  14.3 0.0 copy-done.3
  14.3 0.0 copy-done.4
  14.3 0.2 select_reduce_fusion.1
  14.5 0.6 pad_add_fusion.maps.maps_ref
  15.2 5.0 %pack_rest.1.filled_ref = f32[6,256,16,128]{3,2,1,0:T(8,128)} custom-call(s32[8,128]{1,0:T(8,128)} %pad_add_fusion.maps.maps_ref, f32[2,464,1000]{2,1,0:T(8,128)} %bitcast.3), custom_call_target="tpu_custom_call" | custom-call | bytes 3716096 | tf_op jit(solution)/shard_map/pack_rest/pallas_call | solution.py:445
  20.1 8.5 %weights.1.bank_ref = bf16[5376,1024]{1,0:T(8,128)(2,1)} custom-call(f32[20,20]{1,0:T(8,128)} %up_ref.1, f32[20,20]{1,0:T(8,128)} %down_ref.1), custom_call_target="tpu_custom_call" | custom-call | flops 50000000 | bytes 3200 | tf_op jit(solution)/shard_map/weights/pallas_call | solution.py:445
  28.7 16.2 %all-to-all-done.arrived_ref = f32[256,16,128]{2,1,0:T(8,128)S(1)} async-done(((f32[256,16,128]{2,1,0:T(8,128)}), f32[256,16,128]{2,1,0:T(8,128)S(1)}, u32[]{:S(2)}, u32[]{:S(2)}) %all-to-all-start) | async-done | bytes 2097184 | tf_op jit(solution)/shard_map/all_to_all | solution.py:466
  44.9 2.5 up.3
  47.3 37.1 %all_to_all.40.arrived_ref = f32[256,16,128]{2,1,0:T(8,128)S(1)} all-to-all(f32[256,16,128]{2,1,0:T(8,128)S(1)} %get-tuple-element.17), channel_id=1, replica_groups={{0,59,118,49,108,39,98,29,88,19,78,9,68,127,58,117,48,107,38,97,28,87,1..., dimensions={0} | all-to-all | bytes 4194304 | tf_op jit(solution)/shard_map/all_to_all | solution.py:466
  84.4 2.5 up.4
  87.0 37.2 %all_to_all.41.arrived_ref = f32[256,16,128]{2,1,0:T(8,128)S(1)} all-to-all(f32[256,16,128]{2,1,0:T(8,128)S(1)} %get-tuple-element.19), channel_id=1, replica_groups={{0,59,118,49,108,39,98,29,88,19,78,9,68,127,58,117,48,107,38,97,28,87,1..., dimensions={0} | all-to-all | bytes 4194304 | tf_op jit(solution)/shard_map/all_to_all | solution.py:466
  124.2 2.5 up.5
  126.6 37.1 %all_to_all.42.arrived_ref = f32[256,16,128]{2,1,0:T(8,128)S(1)} all-to-all(f32[256,16,128]{2,1,0:T(8,128)S(1)} %get-tuple-element.21), channel_id=1, replica_groups={{0,59,118,49,108,39,98,29,88,19,78,9,68,127,58,117,48,107,38,97,28,87,1..., dimensions={0} | all-to-all | bytes 4194304 | tf_op jit(solution)/shard_map/all_to_all | solution.py:466
  163.8 4.2 %top.1 = f32[256,16,128]{2,1,0:T(8,128)S(1)} custom-call(f32[256,16,128]{2,1,0:T(8,128)S(1)} %all_to_all.42.arrived_ref, s32[8,128]{1,0:T(8,128)S(1)} %copy-done.1, bf16[5376,1024]{1,0:T(8,128)(2,1)} %weights.1.bank_ref), custom_call_target="tpu_custom_call" | custom-call | flops 1200000000 | bytes 24121344 | tf_op jit(solution)/shard_map/top/pallas_call | solution.py:445
  167.9 0.0 copy-start
  167.9 1.3 copy-done
  169.2 6.8 %all-to-all-start.4 = ((f32[256,16,128]{2,1,0:T(8,128)}), f32[256,16,128]{2,1,0:T(8,128)S(1)}, u32[]{:S(2)}, u32[]{:S(2)}) async-start(f32[256,16,128]{2,1,0:T(8,128)} %copy-done), calls=%async_computation.4 | async-start | bytes 4194304 | tf_op jit(solution)/shard_map/all_to_all | solution.py:466
  176.1 13.5 %base.1.base_ref = f32[9,640,512]{2,1,0:T(8,128)} custom-call(bf16[5376,1024]{1,0:T(8,128)(2,1)} %weights.1.bank_ref, bf16[10496,512]{1,0:T(8,128)(2,1)} %get-tuple-element.22.splits_ref), custom_call_target="tpu_custom_call" | custom-call | flops 3600000000 | bytes 43515904 | tf_op jit(solution)/shard_map/base/pallas_call | solution.py:445
  189.6 17.0 %all-to-all-done.4.returned_ref = f32[256,16,128]{2,1,0:T(8,128)S(1)} async-done(((f32[256,16,128]{2,1,0:T(8,128)}), f32[256,16,128]{2,1,0:T(8,128)S(1)}, u32[]{:S(2)}, u32[]{:S(2)}) %all-to-all-start.4) | async-done | bytes 2097184 | tf_op jit(solution)/shard_map/all_to_all | solution.py:466
  206.7 3.0 down.3
  209.6 37.1 %all_to_all.43.returned_ref = f32[256,16,128]{2,1,0:T(8,128)S(1)} all-to-all(f32[256,16,128]{2,1,0:T(8,128)S(1)} %get-tuple-element.23), channel_id=1, replica_groups={{0,59,118,49,108,39,98,29,88,19,78,9,68,127,58,117,48,107,38,97,28,87,1..., dimensions={0} | all-to-all | bytes 4194304 | tf_op jit(solution)/shard_map/all_to_all | solution.py:466
  246.7 3.0 down.4
  249.7 37.2 %all_to_all.44.returned_ref = f32[256,16,128]{2,1,0:T(8,128)S(1)} all-to-all(f32[256,16,128]{2,1,0:T(8,128)S(1)} %get-tuple-element.25), channel_id=1, replica_groups={{0,59,118,49,108,39,98,29,88,19,78,9,68,127,58,117,48,107,38,97,28,87,1..., dimensions={0} | all-to-all | bytes 4194304 | tf_op jit(solution)/shard_map/all_to_all | solution.py:466
  286.9 3.0 down.5
  289.9 37.1 %all_to_all.45.returned_ref = f32[256,16,128]{2,1,0:T(8,128)S(1)} all-to-all(f32[256,16,128]{2,1,0:T(8,128)S(1)} %get-tuple-element.27), channel_id=1, replica_groups={{0,59,118,49,108,39,98,29,88,19,78,9,68,127,58,117,48,107,38,97,28,87,1..., dimensions={0} | all-to-all | bytes 4194304 | tf_op jit(solution)/shard_map/all_to_all | solution.py:466
  327.0 1.8 store.1
  (2 shorter events, 0.0 us)
Async XLA Ops:
  2.7 11.5 %copy-start.2 = (s32[4,256]{1,0:T(4,128)S(1)}, s32[4,256]{1,0:T(4,128)}, u32[]{:S(2)}) copy-start(s32[4,256]{1,0:T(4,128)} %send_ref.1) | copy-start | bytes 12292
  2.8 11.5 %copy-start.3 = (s32[4,256]{1,0:T(4,128)S(1)}, s32[4,256]{1,0:T(4,128)}, u32[]{:S(2)}) copy-start(s32[4,256]{1,0:T(4,128)} %param.9) | copy-start | bytes 12292
  2.8 11.5 %copy-start.4 = (s32[256]{0:T(256)S(1)}, s32[256]{0:T(256)}, u32[]{:S(2)}) copy-start(s32[256]{0:T(256)} %constant.6) | copy-start | bytes 3076
  2.8 42.1 %all-to-all-start = ((f32[256,16,128]{2,1,0:T(8,128)}), f32[256,16,128]{2,1,0:T(8,128)S(1)}, u32[]{:S(2)}, u32[]{:S(2)}) async-start(f32[256,16,128]{2,1,0:T(8,128)} %pack_first.1), calls=%async_computation | async-start | bytes 4194304 | tf_op jit(solution)/shard_map/all_to_all | solution.py:466
  20.1 24.8 %copy-start.1 = (s32[8,128]{1,0:T(8,128)S(1)}, s32[8,128]{1,0:T(8,128)}, u32[]{:S(2)}) copy-start(s32[8,128]{1,0:T(8,128)} %pad_add_fusion.maps.maps_ref) | copy-start | bytes 12292
  167.9 1.3 copy-start
  169.2 37.4 %all-to-all-start.4 = ((f32[256,16,128]{2,1,0:T(8,128)}), f32[256,16,128]{2,1,0:T(8,128)S(1)}, u32[]{:S(2)}, u32[]{:S(2)}) async-start(f32[256,16,128]{2,1,0:T(8,128)} %copy-done), calls=%async_computation.4 | async-start | bytes 4194304 | tf_op jit(solution)/shard_map/all_to_all | solution.py:466

commit v3 on v1

--- a/solution.py
+++ b/solution.py
@@ -402,13 +402,13 @@
         for i, value in enumerate(windows(chunks)):
             start = (n * DEGREE + i) * ROWS
             high[start : start + ROWS, :], low[start : start + ROWS, :] = split(value)
+    for copy in copies[1:3]:
+        copy.wait()
+    values = down_product(high[...], low[...], weights)
     start, number = leaf_range(height + 1)
     gather_leaves(height + 1, 0, maps, returned_ref, flat_leaves, rows, number)
     store = pltpu.make_async_copy(rows, result_ref.at[:, start : start + number, :], sems.at[4])
     store.start()
-    for copy in copies[1:3]:
-        copy.wait()
-    values = down_product(high[...], low[...], weights)
     copies[3].wait()
     depth = WIDE // COUNT
     keep(refined, [base[n * depth : (n + 1) * depth, :] + values[n] for n in range(COUNT)])
@@ -459,8 +459,8 @@
     return lax.all_to_all(blocks, "dev", split_axis=0, concat_axis=0, tiled=True)
 
 
-def flat(number):
-    return pltpu.VMEM((number * HEIGHT, 128), f32)
+def flat(number, spare=HEIGHT):
+    return pltpu.VMEM((number * HEIGHT + spare, 128), f32)
 
 
 def halves(*dims):
@@ -476,7 +476,7 @@
         self.orbital = orbital
         self.rows = rows
         self.slots = shape(SLOTS, HEIGHT, 128)
-        self.placed = pltpu.VMEM((COUNT * 8 * 8 * ROWS, 128), f32)
+        self.placed = pltpu.VMEM((COUNT * 8 * 8 * ROWS + ROWS, 128), f32)
         self.going = call(
             functools.partial(first_kernel, orbital),
             self.slots,
@@ -545,7 +545,7 @@
         )
 
     def top(self, height):
-        scratch = [self.maps_smem] + halves((WIDE, 512)) + [self.placed, pltpu.VMEM((WIDE, 512), f32), flat(PER)]
+        scratch = [self.maps_smem] + halves((WIDE, 512)) + [self.placed, pltpu.VMEM((WIDE, 512), f32), flat(PER, 8 * HEIGHT)]
         scratch += single((512, 1024), (320, 1024)) + [DMA((3,))]
         self.going = call(
             functools.partial(top_kernel, height),
@@ -560,8 +560,8 @@
 
     def down(self, height, result):
         number = leaf_range(height + 1)[1]
-        scratch = [self.maps_smem, pltpu.VMEM((WIDE, 512), f32), pltpu.VMEM((COUNT * 8 * ROWS, 128), f32)]
-        scratch += halves((WIDE // 2, 128)) + [pltpu.VMEM((WIDE, 512), f32), flat(PER)]
+        scratch = [self.maps_smem, pltpu.VMEM((WIDE, 512), f32), pltpu.VMEM((COUNT * 8 * ROWS + ROWS, 128), f32)]
+        scratch += halves((WIDE // 2, 128)) + [pltpu.VMEM((WIDE, 512), f32), flat(PER, 8 * HEIGHT)]
         scratch += [flat(number), pltpu.VMEM((COUNT, number, CELLS), f32)]
         scratch += single((256, 1024), (320, 512)) + [DMA((5,))]
         operands = (self.arrived, self.maps, self.bases, self.bank)

time: 311 us -> 311 us (level)
  no operation moved by 1% of the time
where the time goes in v3:
time: 311 us
  blocking collectives  206 us (66%)
  Pallas kernels  52.9 us (17%)
  waiting for transfers between devices  33.2 us (11%)
  starting transfers between devices  15.9 us (5%)
    all_to_all x6, blocking collectives, exchange(): lax.all_to_all(blocks, 'dev', split_axis=0, concat_axis=0, tiled=True)  206 us
    pallas_call x12, Pallas kernels, call(): pl.pallas_call(kernel, out_shape=out_shape, in_specs=in_specs, out_specs=...  52.9 us
    all_to_all x2, waiting for transfers between devices, exchange(): lax.all_to_all(blocks, 'dev', split_axis=0, concat_axis=0, tiled=True)  33.2 us
    all_to_all x2, starting transfers between devices, exchange(): lax.all_to_all(blocks, 'dev', split_axis=0, concat_axis=0, tiled=True)  15.9 us
  transfers between devices with their start and end apart: 2, of which 2 were waited for; matrix products, arithmetic and copies ran while one was open for 0% of the time, Pallas kernels for 9%

profile of v3, /device:TPU:1, one launch (start us, length us, event | category | flops | bytes accessed | tf_op | source)
XLA Modules:
  0.0 310.8 jit_solution(7220704348350811993)
XLA Ops:
  0.0 2.7 pack_first.1
  2.7 0.0 copy-start.2
  2.8 0.0 copy-start.3
  2.8 11.5 %all-to-all-start = ((f32[256,16,128]{2,1,0:T(8,128)}), f32[256,16,128]{2,1,0:T(8,128)S(1)}, u32[]{:S(2)}, u32[]{:S(2)}) async-start(f32[256,16,128]{2,1,0:T(8,128)} %pack_first.1), calls=%async_computation | async-start | bytes 4194304 | tf_op jit(solution)/shard_map/all_to_all | solution.py:459
  14.3 0.0 copy-done.2
  14.3 0.0 copy-done.3
  14.3 0.2 select_reduce_fusion
  14.5 0.6 pad_add_fusion.maps.maps_ref
  15.1 5.0 %pack_rest.1.filled_ref = f32[6,256,16,128]{3,2,1,0:T(8,128)} custom-call(s32[8,128]{1,0:T(8,128)} %pad_add_fusion.maps.maps_ref, f32[2,464,1000]{2,1,0:T(8,128)} %bitcast.3), custom_call_target="tpu_custom_call" | custom-call | bytes 3716096 | tf_op jit(solution)/shard_map/pack_rest/pallas_call | solution.py:440
  20.1 0.0 copy-start.1
  20.1 8.5 %weights.1.bank_ref = bf16[5376,1024]{1,0:T(8,128)(2,1)} custom-call(f32[20,20]{1,0:T(8,128)} %up_ref.1, f32[20,20]{1,0:T(8,128)} %down_ref.1), custom_call_target="tpu_custom_call" | custom-call | flops 50000000 | bytes 3200 | tf_op jit(solution)/shard_map/weights/pallas_call | solution.py:440
  28.7 16.1 %all-to-all-done.arrived_ref = f32[256,16,128]{2,1,0:T(8,128)S(1)} async-done(((f32[256,16,128]{2,1,0:T(8,128)}), f32[256,16,128]{2,1,0:T(8,128)S(1)}, u32[]{:S(2)}, u32[]{:S(2)}) %all-to-all-start) | async-done | bytes 2097184 | tf_op jit(solution)/shard_map/all_to_all | solution.py:459
  44.8 0.0 copy-done.1
  44.8 2.4 up.3
  47.3 34.4 %all_to_all.40.arrived_ref = f32[256,16,128]{2,1,0:T(8,128)S(1)} all-to-all(f32[256,16,128]{2,1,0:T(8,128)S(1)} %get-tuple-element.17), channel_id=1, replica_groups=mesh['dev'=128] {'dev'}, dimensions={0} | all-to-all | bytes 4194304 | tf_op jit(solution)/shard_map/all_to_all | solution.py:459
  81.6 2.5 up.4
  84.2 34.4 %all_to_all.41.arrived_ref = f32[256,16,128]{2,1,0:T(8,128)S(1)} all-to-all(f32[256,16,128]{2,1,0:T(8,128)S(1)} %get-tuple-element.19), channel_id=1, replica_groups=mesh['dev'=128] {'dev'}, dimensions={0} | all-to-all | bytes 4194304 | tf_op jit(solution)/shard_map/all_to_all | solution.py:459
  118.6 2.4 up.5
  121.0 34.4 %all_to_all.42.arrived_ref = f32[256,16,128]{2,1,0:T(8,128)S(1)} all-to-all(f32[256,16,128]{2,1,0:T(8,128)S(1)} %get-tuple-element.21), channel_id=1, replica_groups=mesh['dev'=128] {'dev'}, dimensions={0} | all-to-all | bytes 4194304 | tf_op jit(solution)/shard_map/all_to_all | solution.py:459
  155.4 4.2 %top.1 = f32[256,16,128]{2,1,0:T(8,128)S(1)} custom-call(f32[256,16,128]{2,1,0:T(8,128)S(1)} %all_to_all.42.arrived_ref, s32[8,128]{1,0:T(8,128)S(1)} %copy-done.1, bf16[5376,1024]{1,0:T(8,128)(2,1)} %weights.1.bank_ref), custom_call_target="tpu_custom_call" | custom-call | flops 1200000000 | bytes 24121344 | tf_op jit(solution)/shard_map/top/pallas_call | solution.py:440
  159.6 0.0 copy-start
  159.6 1.3 copy-done
  160.9 4.4 %all-to-all-start.4 = ((f32[256,16,128]{2,1,0:T(8,128)}), f32[256,16,128]{2,1,0:T(8,128)S(1)}, u32[]{:S(2)}, u32[]{:S(2)}) async-start(f32[256,16,128]{2,1,0:T(8,128)} %copy-done), calls=%async_computation.4 | async-start | bytes 4194304 | tf_op jit(solution)/shard_map/all_to_all | solution.py:459
  165.3 13.6 %base.1.base_ref = f32[9,640,512]{2,1,0:T(8,128)} custom-call(bf16[5376,1024]{1,0:T(8,128)(2,1)} %weights.1.bank_ref, bf16[10496,512]{1,0:T(8,128)(2,1)} %get-tuple-element.22.splits_ref), custom_call_target="tpu_custom_call" | custom-call | flops 3600000000 | bytes 43515904 | tf_op jit(solution)/shard_map/base/pallas_call | solution.py:440
  178.8 17.1 %all-to-all-done.4.returned_ref = f32[256,16,128]{2,1,0:T(8,128)S(1)} async-done(((f32[256,16,128]{2,1,0:T(8,128)}), f32[256,16,128]{2,1,0:T(8,128)S(1)}, u32[]{:S(2)}, u32[]{:S(2)}) %all-to-all-start.4) | async-done | bytes 2097184 | tf_op jit(solution)/shard_map/all_to_all | solution.py:459
  195.9 3.2 %down.3 = (f32[256,16,128]{2,1,0:T(8,128)S(1)}, f32[2,464,1000]{2,1,0:T(8,128)}) custom-call(f32[256,16,128]{2,1,0:T(8,128)S(1)} %all-to-all-done.4.returned_ref, s32[8,128]{1,0:T(8,128)S(1)} %copy-done.1, f32[9,640,512]{2,1,0:T(8,128)} %base.1.base_ref, bf16[5376,1024]{1,0:T(8,128)(2,1)} %weights.1.bank_ref), custom_call_target="tpu_custom_call" | custom-call | flops 400000000 | bytes 35917824 | tf_op jit(solution)/shard_map/down/pallas_call | solution.py:440
  199.2 34.4 %all_to_all.43.returned_ref = f32[256,16,128]{2,1,0:T(8,128)S(1)} all-to-all(f32[256,16,128]{2,1,0:T(8,128)S(1)} %get-tuple-element.23), channel_id=1, replica_groups=mesh['dev'=128] {'dev'}, dimensions={0} | all-to-all | bytes 4194304 | tf_op jit(solution)/shard_map/all_to_all | solution.py:459
  233.6 3.2 %down.4 = (f32[256,16,128]{2,1,0:T(8,128)S(1)}, f32[2,464,1000]{2,1,0:T(8,128)}) custom-call(f32[256,16,128]{2,1,0:T(8,128)S(1)} %all_to_all.43.returned_ref, s32[8,128]{1,0:T(8,128)S(1)} %copy-done.1, f32[9,640,512]{2,1,0:T(8,128)} %base.1.base_ref, bf16[5376,1024]{1,0:T(8,128)(2,1)} %weights.1.bank_ref, ...), custom_call_target="tpu_custom_call", output_to_operand_aliasing={{1}: (4, {})} | custom-call | flops 400000000 | bytes 39629824 | tf_op jit(solution)/shard_map/down/pallas_call | solution.py:440
  236.8 34.4 %all_to_all.44.returned_ref = f32[256,16,128]{2,1,0:T(8,128)S(1)} all-to-all(f32[256,16,128]{2,1,0:T(8,128)S(1)} %get-tuple-element.25), channel_id=1, replica_groups=mesh['dev'=128] {'dev'}, dimensions={0} | all-to-all | bytes 4194304 | tf_op jit(solution)/shard_map/all_to_all | solution.py:459
  271.2 3.2 %down.5 = (f32[256,16,128]{2,1,0:T(8,128)S(1)}, f32[2,464,1000]{2,1,0:T(8,128)}) custom-call(f32[256,16,128]{2,1,0:T(8,128)S(1)} %all_to_all.44.returned_ref, s32[8,128]{1,0:T(8,128)S(1)} %copy-done.1, f32[9,640,512]{2,1,0:T(8,128)} %base.1.base_ref, bf16[5376,1024]{1,0:T(8,128)(2,1)} %weights.1.bank_ref, ...), custom_call_target="tpu_custom_call", output_to_operand_aliasing={{1}: (4, {})} | custom-call | flops 400000000 | bytes 39629824 | tf_op jit(solution)/shard_map/down/pallas_call | solution.py:440
  274.5 34.4 %all_to_all.45.returned_ref = f32[256,16,128]{2,1,0:T(8,128)S(1)} all-to-all(f32[256,16,128]{2,1,0:T(8,128)S(1)} %get-tuple-element.27), channel_id=1, replica_groups=mesh['dev'=128] {'dev'}, dimensions={0} | all-to-all | bytes 4194304 | tf_op jit(solution)/shard_map/all_to_all | solution.py:459
  308.8 1.8 store.1
Async XLA Ops:
  2.7 11.5 %copy-start.2 = (s32[4,256]{1,0:T(4,128)S(1)}, s32[4,256]{1,0:T(4,128)}, u32[]{:S(2)}) copy-start(s32[4,256]{1,0:T(4,128)} %send_ref.1) | copy-start | bytes 12292
  2.8 11.5 %copy-start.3 = (s32[4,256]{1,0:T(4,128)S(1)}, s32[4,256]{1,0:T(4,128)}, u32[]{:S(2)}) copy-start(s32[4,256]{1,0:T(4,128)} %param.7) | copy-start | bytes 12292
  2.8 42.0 %all-to-all-start = ((f32[256,16,128]{2,1,0:T(8,128)}), f32[256,16,128]{2,1,0:T(8,128)S(1)}, u32[]{:S(2)}, u32[]{:S(2)}) async-start(f32[256,16,128]{2,1,0:T(8,128)} %pack_first.1), calls=%async_computation | async-start | bytes 4194304 | tf_op jit(solution)/shard_map/all_to_all | solution.py:459
  20.1 24.7 %copy-start.1 = (s32[8,128]{1,0:T(8,128)S(1)}, s32[8,128]{1,0:T(8,128)}, u32[]{:S(2)}) copy-start(s32[8,128]{1,0:T(8,128)} %pad_add_fusion.maps.maps_ref) | copy-start | bytes 12292
  159.6 1.3 copy-start
  160.9 35.0 %all-to-all-start.4 = ((f32[256,16,128]{2,1,0:T(8,128)}), f32[256,16,128]{2,1,0:T(8,128)S(1)}, u32[]{:S(2)}, u32[]{:S(2)}) async-start(f32[256,16,128]{2,1,0:T(8,128)} %copy-done), calls=%async_computation.4 | async-start | bytes 4194304 | tf_op jit(solution)/shard_map/all_to_all | solution.py:459
